TPU v7x, 512 devices: a whole 4x4x16 slice. The times are simulated.
512 devices in a mesh: dp: 16 (over z), seq: 32 (over x, y, core).
Axes of the slice: x: 4, y: 4, z: 16, core: 2. Of those that a mesh axis runs over, the one named last changes fastest.
Arguments:
- hidden_states: bfloat16 [1024, 128, 1152], P(('dp', 'seq')), may hold values from -6 to 6
- spatial_qkv: bfloat16 [1024, 128, 3456], P(('dp', 'seq')), may hold values from -6 to 6
- spatial_out_weight: bfloat16 [1152, 1152], P('dp'), may hold values from -0.1875 to 0.1875
- temporal_qkv_weight: bfloat16 [1152, 3456], P('dp'), may hold values from -1 to 1, as said below
- modulation: float32 [4, 1152], replicated, may hold values from -4 to 4
- video_ids: int32 [1024], P(('dp', 'seq')), may hold values from 0 to 63, never falling along the last dimension, each value on 1 to 64 neighbouring positions
Outputs:
- block_output: bfloat16 [1024, 128, 1152], P(('dp', 'seq'))
Inputs may be any that keep to these rules, and one draw needn't show every extreme that they name: `video_ids`: frames of one video are consecutive; a video has 1 to 64 frames, and some video has exactly 64. `temporal_qkv_weight`: a matrix scaled by the square root of its fan-in 1152.
All inputs are finite; a program needn't handle non-finite values.
Results may differ from a plain program's by a relative error of at most 0.04.
Values may be sent and summed in bfloat16 or wider, within the bound.
A program may use at most 64 MiB of HBM per device.

v0:
```python
import math

import jax
import jax.numpy as jnp
from jax import lax
from jax.sharding import PartitionSpec as P

HEADS = 16
HD = 72


NEG = -1e30
EPS = 1e-06


def with_halo(block, sides, width):
    for axis, dim in sides:
        count = lax.axis_size(axis)
        forward = [(i, i + 1) for i in range(count - 1)]
        backward = [(target, source) for source, target in forward]
        low = lax.ppermute(
            lax.slice_in_dim(block, block.shape[dim] - width, None, axis=dim), axis, forward
        )
        high = lax.ppermute(lax.slice_in_dim(block, 0, width, axis=dim), axis, backward)
        block = jnp.concatenate([low, block, high], axis=dim)
    return block


def softmax_weights(scores):
    top = jnp.max(scores, axis=-1, keepdims=True)
    powers = jnp.exp(scores - top)
    return (powers / jnp.sum(powers, axis=-1, keepdims=True)).astype(jnp.bfloat16)


def add_rows(left, piece):
    return jnp.dot(left, piece, preferred_element_type=jnp.float32)


def shards(
    hidden_states, spatial_qkv, spatial_out_weight, temporal_qkv_weight, modulation, video_ids
):
    frames_dev, patches, triple = spatial_qkv.shape
    width = triple // 3
    seq_count = lax.axis_size("seq")
    group_frames = frames_dev * seq_count
    local_patches = patches // seq_count
    scale = 1.0 / math.sqrt(HD)
    parts = spatial_qkv.reshape(frames_dev, patches, 3, HEADS, HD)
    scores = (
        jnp.einsum(
            "fqhd,fkhd->fhqk", parts[:, :, 0], parts[:, :, 1], preferred_element_type=jnp.float32
        )
        * scale
    )
    weights = softmax_weights(scores)
    spatial = jnp.einsum(
        "fhqk,fkhd->fqhd", weights, parts[:, :, 2], preferred_element_type=jnp.float32
    )
    spatial = spatial.astype(jnp.bfloat16).reshape(frames_dev * patches, width)
    projected = add_rows(spatial, lax.all_gather(spatial_out_weight, "dp", axis=0, tiled=True))
    residual = (
        hidden_states.reshape(-1, width).astype(jnp.float32) + modulation[0] * projected
    ).astype(jnp.bfloat16)
    values32 = residual.astype(jnp.float32)
    centred = values32 - jnp.mean(values32, axis=-1, keepdims=True)
    variance = jnp.mean(centred * centred, axis=-1, keepdims=True)
    normed = (centred * lax.rsqrt(variance + EPS) * (1.0 + modulation[2]) + modulation[1]).astype(
        jnp.bfloat16
    )
    result = add_rows(normed, lax.all_gather(temporal_qkv_weight, "dp", axis=0, tiled=True))
    local_qkv = result.astype(jnp.bfloat16).reshape(frames_dev, patches, triple)
    temporal_qkv = lax.all_to_all(local_qkv, "seq", split_axis=1, concat_axis=0, tiled=True)
    group_ids = lax.all_gather(video_ids + 1, "seq", axis=0, tiled=True)
    key_ids = with_halo(group_ids, (("dp", 0),), group_frames)
    queries = temporal_qkv[:, :, :width].reshape(group_frames, local_patches, HEADS, HD)
    keyvals = with_halo(temporal_qkv[:, :, width:], (("dp", 0),), group_frames)
    keys = keyvals[:, :, :width].reshape(3 * group_frames, local_patches, HEADS, HD)
    values = keyvals[:, :, width:].reshape(3 * group_frames, local_patches, HEADS, HD)
    scores = (
        jnp.einsum("iphd,jphd->phij", queries, keys, preferred_element_type=jnp.float32) * scale
    )
    same = group_ids[:, None] == key_ids[None, :]
    scores = jnp.where(same[None, None], scores, NEG)
    weights = softmax_weights(scores)
    temporal = jnp.einsum("phij,jphd->iphd", weights, values, preferred_element_type=jnp.float32)
    temporal = temporal.astype(jnp.bfloat16).reshape(group_frames, local_patches, width)
    returned = lax.all_to_all(temporal, "seq", split_axis=0, concat_axis=1, tiled=True)
    output = residual.astype(jnp.float32) + modulation[3] * returned.reshape(-1, width).astype(
        jnp.float32
    )
    return output.astype(jnp.bfloat16).reshape(frames_dev, patches, width)


def solution(mesh):
    in_specs = (
        P(("dp", "seq"), None, None),
        P(("dp", "seq"), None, None),
        P("dp", None),
        P("dp", None),
        P(),
        P(("dp", "seq")),
    )
    out_specs = P(("dp", "seq"), None, None)
    return jax.shard_map(shards, mesh=mesh, in_specs=in_specs, out_specs=out_specs, check_vma=False)
```

profile of v0, /device:TPU:1, one launch (start us, length us, event | category | flops | bytes accessed | tf_op | source)
XLA Modules:
  0.0 314.8 jit_solution(6235739868157123804)
XLA Ops:
  8.0 2.8 copy.37
  10.8 2.2 fusion.28
  13.0 2.1 fusion.13
  15.8 64.9 %all-gather.3.cloned.1.call-done = bf16[1152,1152]{1,0:T(8,128)(2,1)} async-done(((bf16[72,1152]{1,0:T(8,128)(2,1)}), bf16[1152,1152]{1,0:T(8,128)(2,1)}) %all-gather.3.cloned.1.call-update) | async-done | bytes 2654224 | tf_op jit(solution)/shard_map/all_gather | solution.py:60
  80.7 2.9 fusion.29
  83.9 106.2 %all-gather.5.cloned.1.call-done = bf16[1152,3456]{1,0:T(8,128)(2,1)} async-done(((bf16[72,3456]{1,0:T(8,128)(2,1)}), bf16[1152,3456]{1,0:T(8,128)(2,1)}) %all-gather.5.cloned.1.call-update) | async-done | bytes 7962640 | tf_op jit(solution)/shard_map/all_gather | solution.py:70
  190.1 5.9 %convolution_convert_fusion = bf16[256,3456]{1,0:T(8,128)(2,1)S(1)} fusion(bf16[1152,3456]{1,0:T(8,128)(2,1)} %all-gather.5.cloned.1.call-done, f32[256,1152]{1,0:T(8,128)S(1)} %get-tuple-element.14, f32[1152]{0:T(1024)S(1)} %get-tuple-element.7, f32[1152]{0:T(1024)S(1)} %get-tuple-element.8, f32[256]{0:T(256)S(1)} %add_rsqrt_fusion, ...), kind=kOutput, calls=%fused_computation.2 | convolution fusion | flops 2040791040 | bytes 10923008 | tf_op jit(solution)/shard_map/dot_general | solution.py:36
  196.0 1.8 copy.43
  197.8 32.2 %all_to_all.27 = bf16[2,128,3456]{2,0,1:T(2,128)(2,1)S(1)} all-to-all(bf16[2,128,3456]{2,0,1:T(2,128)(2,1)S(1)} %copy.43), channel_id=1, replica_groups=mesh['dp'=16,'seq'=32] {'seq'}, dimensions={1} | all-to-all | bytes 3538944 | tf_op jit(solution)/shard_map/all_to_all | solution.py:72
  230.7 1.4 slice.47
  232.1 2.3 collective-permute-start
  237.7 11.0 %all-reduce = s32[64]{0:T(128)S(1)} all-reduce(s32[64]{0:T(128)S(1)} %add_dynamic-update-slice_fusion), channel_id=1, replica_groups=mesh['dp'=16,'seq'=32] {'seq'}, use_global_device_ids=true, to_apply=%add | all-reduce | flops 64 | bytes 512
  248.8 4.0 %collective-permute-start.2 = (s32[64]{0:T(128)S(1)}, s32[64]{0:T(128)S(1)}, u32[]{:S(2)}, u32[]{:S(2)}) collective-permute-start(s32[64]{0:T(128)S(1)} %all-reduce), channel_id=1, source_target_pairs={{0,32},{32,64},{64,96},{96,128},{128,160},{160,192},{192,224},{224... | collective-permute-start | bytes 776 | tf_op jit(solution)/shard_map/ppermute | solution.py:21
  252.8 1.5 collective-permute-start.3
  254.3 5.1 %collective-permute-done.2 = s32[64]{0:T(128)S(1)} collective-permute-done((s32[64]{0:T(128)S(1)}, s32[64]{0:T(128)S(1)}, u32[]{:S(2)}, u32[]{:S(2)}) %collective-permute-start.2) | collective-permute-done | bytes 288 | tf_op jit(solution)/shard_map/ppermute | solution.py:21
  259.4 4.9 %collective-permute-done.3 = s32[64]{0:T(128)S(1)} collective-permute-done((s32[64]{0:T(128)S(1)}, s32[64]{0:T(128)S(1)}, u32[]{:S(2)}, u32[]{:S(2)}) %collective-permute-start.3) | collective-permute-done | bytes 288 | tf_op jit(solution)/shard_map/ppermute | solution.py:24
  264.7 1.9 reshape.92
  266.6 4.1 %pad_maximum_fusion = bf16[192,4,2304]{2,1,0:T(4,128)(2,1)S(1)} fusion(bf16[64,4,2304]{2,1,0:T(4,128)(2,1)} %collective-permute-done.1, bf16[64,4,2304]{2,1,0:T(4,128)(2,1)} %slice.47, bf16[64,4,2304]{2,1,0:T(4,128)(2,1)} %collective-permute-done), kind=kLoop, calls=%fused_computation.6 | loop fusion | flops 3538944 | bytes 7077888 | tf_op jit(solution)/shard_map/concatenate | solution.py:25
  270.8 3.0 fusion.27
  273.8 3.8 %copy.47 = bf16[192,4,1152]{0,2,1:T(8,128)(2,1)S(1)} copy(bf16[192,4,1152]{2,1,0:T(4,128)(2,1)} %get-tuple-element.9) | data formatting | bytes 3538944 | tf_op jit(solution)/shard_map/slice | solution.py:77
  277.6 4.9 %copy.45 = bf16[192,4,1152]{0,2,1:T(8,128)(2,1)} copy(bf16[192,4,1152]{2,1,0:T(4,128)(2,1)} %get-tuple-element.10) | data formatting | bytes 3538944 | tf_op jit(solution)/shard_map/slice | solution.py:78
  283.8 2.1 fusion.30
  287.7 1.7 reshape.93
  289.4 16.2 %all_to_all.28 = bf16[64,4,1152]{2,1,0:T(4,128)(2,1)S(1)} all-to-all(bf16[64,4,1152]{2,1,0:T(4,128)(2,1)S(1)} %reshape.93), channel_id=1, replica_groups=mesh['dp'=16,'seq'=32] {'seq'}, dimensions={0} | all-to-all | bytes 1179648 | tf_op jit(solution)/shard_map/all_to_all | solution.py:87
  (38 shorter events, 11.4 us)
Async XLA Ops:
  6.5 74.2 %all-gather.3.cloned.1.call-start = ((), (), s32[]{:S(2)}) async-start(), calls=%async_computation.2 | async-start | bytes 2820096 | tf_op jit(solution)/shard_map/all_gather | solution.py:60
  7.3 182.8 %all-gather.5.cloned.1.call-start = ((), (), s32[]{:S(2)}) async-start(), calls=%async_computation.3 | async-start | bytes 8460288 | tf_op jit(solution)/shard_map/all_gather | solution.py:70
  13.0 2.8 copy-start.3
  13.0 67.7 %copy-start.4 = (bf16[2,128,1152]{2,1,0:T(8,128)(2,1)S(1)}, bf16[2,128,1152]{2,1,0:T(8,128)(2,1)}, u32[]{:S(2)}) copy-start(bf16[2,128,1152]{2,1,0:T(8,128)(2,1)} %param.6) | copy-start | bytes 1769476
  83.6 112.4 %copy-start = (f32[256,1152]{1,0:T(8,128)}, f32[256,1152]{1,0:T(8,128)S(1)}, u32[]{:S(2)}) copy-start(f32[256,1152]{1,0:T(8,128)S(1)} %get-tuple-element.14) | copy-start | bytes 3538948
  230.0 7.6 %copy-start.5 = (s32[2]{0:T(128)S(1)}, s32[2]{0:T(128)}, u32[]{:S(2)}) copy-start(s32[2]{0:T(128)} %param.11) | copy-start | bytes 28
  232.1 34.5 %collective-permute-start = (bf16[64,4,2304]{2,1,0:T(4,128)(2,1)}, bf16[64,4,2304]{2,1,0:T(4,128)(2,1)}, u32[]{:S(2)}, u32[]{:S(2)}) collective-permute-start(bf16[64,4,2304]{2,1,0:T(4,128)(2,1)} %slice.47), channel_id=1, source_target_pairs={{0,32},{32,64},{64,96},{96,128},{128,160},{160,192},{192,224},{224... | collective-permute-start | bytes 3538952 | tf_op jit(solution)/shard_map/ppermute | solution.py:21
  234.4 32.2 %collective-permute-start.1 = (bf16[64,4,2304]{2,1,0:T(4,128)(2,1)}, bf16[64,4,2304]{2,1,0:T(4,128)(2,1)}, u32[]{:S(2)}, u32[]{:S(2)}) collective-permute-start(bf16[64,4,2304]{2,1,0:T(4,128)(2,1)} %slice.47), channel_id=1, source_target_pairs={{32,0},{64,32},{96,64},{128,96},{160,128},{192,160},{224,192},{256... | collective-permute-start | bytes 3538952 | tf_op jit(solution)/shard_map/ppermute | solution.py:24
  248.8 10.6 %collective-permute-start.2 = (s32[64]{0:T(128)S(1)}, s32[64]{0:T(128)S(1)}, u32[]{:S(2)}, u32[]{:S(2)}) collective-permute-start(s32[64]{0:T(128)S(1)} %all-reduce), channel_id=1, source_target_pairs={{0,32},{32,64},{64,96},{96,128},{128,160},{160,192},{192,224},{224... | collective-permute-start | bytes 776 | tf_op jit(solution)/shard_map/ppermute | solution.py:21
  252.8 11.5 %collective-permute-start.3 = (s32[64]{0:T(128)S(1)}, s32[64]{0:T(128)S(1)}, u32[]{:S(2)}, u32[]{:S(2)}) collective-permute-start(s32[64]{0:T(128)S(1)} %all-reduce), channel_id=1, source_target_pairs={{32,0},{64,32},{96,64},{128,96},{160,128},{192,160},{224,192},{256... | collective-permute-start | bytes 776 | tf_op jit(solution)/shard_map/ppermute | solution.py:24
  283.8 2.1 copy-start.2
  305.7 1.3 copy-start.1
Sparse Core Ops, SparseCore 0:
  9.4 71.2 all-gather.2
  82.8 107.2 all-gather.4
where the time goes:
time: 315 us
  waiting for transfers between devices  183 us (58%)
  blocking collectives  59.4 us (19%)
  local copies, waits for them, and re-layouts  26 us (8%)
  matrix products  15.6 us (5%)
  between operations  14.3 us (5%)
  starting transfers between devices  9.1 us (3%)
  other arithmetic  7.82 us (2%)
    all_gather x1, waiting for transfers between devices, shards(): lax.all_gather(temporal_qkv_weight, 'dp', axis=0, tiled=True)  106 us
    all_gather x1, waiting for transfers between devices, shards(): lax.all_gather(spatial_out_weight, 'dp', axis=0, tiled=True)  64.9 us
    all_to_all x1, blocking collectives, shards(): lax.all_to_all(local_qkv, 'seq', split_axis=1, concat_axis=0, tiled=True)  32.2 us
    all_to_all x1, blocking collectives, shards(): lax.all_to_all(temporal, 'seq', split_axis=0, concat_axis=1, tiled=True)  16.2 us
    unnamed x1, blocking collectives  11 us
    dot_general x2, matrix products, add_rows(): return jnp.dot(left, piece, preferred_element_type=jnp.float32)  8.84 us
    slice x2, local copies, waits for them, and re-layouts, shards(): keyvals[:, :, :width].reshape(3 * group_frames, local_patches, HEADS, HD)  6.78 us
    ppermute x2, starting transfers between devices, with_halo(): lax.ppermute(lax.slice_in_dim(block, block.shape[dim] - width, None, axis...  6.31 us
  transfers between devices with their start and end apart: 6, of which 4 were waited for; matrix products, arithmetic and copies ran while one was open for 5% of the time, Pallas kernels for 0%

commit v1 on v0

v1 whole, which is shorter than its diff:
```python
import math

import jax
import jax.numpy as jnp
from jax import lax
from jax.experimental import pallas as pl
from jax.experimental.pallas import tpu as pltpu
from jax.sharding import PartitionSpec as P

HEADS = 16
HD = 72
D = 1152
NEG = -1e30
EPS = 1e-06
SCALE = 1.0 / math.sqrt(HD)

NZ = 16
ROWS = 72
CHIPS = 16
POS = 8
BLK = 16
TOK = 1280
HALF = 640
MESH = pl.DeviceIdType.MESH
BF = jnp.bfloat16
F32 = jnp.float32


def iota(shape, dim):
    return lax.broadcasted_iota(jnp.int32, shape, dim)


def dot(a, b):
    return jnp.dot(a, b, preferred_element_type=F32)


def dot_t(a, b):
    return lax.dot_general(a, b, (((1,), (1,)), ((), ())), preferred_element_type=F32)


def softmax(scores):
    top = jnp.max(scores, axis=-1, keepdims=True)
    powers = jnp.exp(scores - top)
    return (powers * (1.0 / jnp.sum(powers, axis=-1, keepdims=True))).astype(BF)


def pair_masks(pair, rows):
    lane = iota((rows, 256), 1)
    low = 16 * pair
    first = (lane >= low) & (lane < low + HD)
    second = (lane >= low + HD) & (lane < low + 2 * HD)
    return first, second


def frame_order(rows):
    core, chip, two, pos = rows // 256, (rows % 256) // 16, (rows % 16) // 8, rows % 8
    return pos * 64 + chip * 4 + core * 2 + two


def kernel(
    hid_ref, qkv_ref, wo_ref, wt_ref, mod_ref, ids_ref, out_ref,
    w8, wxo, wxq, wout, wqkv, sp, res, ns, xb, xp, qs, kv, tt, tb, rb, perm, perm_t,
    zs, zr, xso, xro, xsq, xrq, ls, lr, a_s, a_r, hs, hr, ss, sr, r_s, r_r,
):
    z, seq = lax.axis_index("dp"), lax.axis_index("seq")
    core, chip = seq % 2, seq // 2
    x, y = chip // 4, chip % 4
    up, down, sib = (z + 1) % NZ, (z + NZ - 1) % NZ, chip * 2 + (1 - core)

    def copy(src, dst, send, recv, dev):
        return pltpu.make_async_remote_copy(
            src_ref=src, dst_ref=dst, send_sem=send, recv_sem=recv, device_id=dev, device_id_type=MESH
        )

    barrier = pltpu.get_barrier_semaphore()

    def greet(j, _):
        pl.semaphore_signal(barrier, inc=1, device_id=(z, (seq + j) % 32), device_id_type=MESH)
        return 0

    lax.fori_loop(1, 32, greet, 0)
    pl.semaphore_signal(barrier, inc=1, device_id=(up, seq), device_id_type=MESH)
    pl.semaphore_signal(barrier, inc=1, device_id=(down, seq), device_id_type=MESH)

    for q in range(4):
        wxo[core, q, z] = wo_ref[:, pl.ds(pl.multiple_of(256 * q + 128 * core, 128), 128)]
        for u in range(4):
            n = min(4 * q + u, 14)
            lanes = pl.ds(pl.multiple_of((n // 5) * D + 128 * (n % 5) + 512 * core, 128), 128)
            wxq[q, z, :, 128 * u : 128 * u + 128] = wt_ref[:, lanes]
    w8[z] = wo_ref[:, 1024:1152]
    sp[...] = jnp.zeros_like(sp)
    pl.semaphore_wait(barrier, 33)

    def quarter(k):
        odd = k % 2
        return y * (1 - odd) + x * odd

    def ring(kind, way, step, k):
        dev = (up, seq) if way == 0 else (down, seq)
        ref = (wxo.at[core, quarter(k), k], w8.at[k], wxq.at[quarter(k), k])[kind]
        return copy(ref, ref, zs.at[way, kind, step], zr.at[way, kind, step], dev)

    def sent(way, step):
        return (z + NZ - step) % NZ if way == 0 else (z + step) % NZ

    def across(kind, k, j):
        odd = k % 2
        dev = (z, (((x + j * odd) % 4) * 4 + (y + j * (1 - odd)) % 4) * 2 + core)
        q = quarter(k)
        if kind == 0:
            ref, send, recv = wxo.at[core, q, k], xso.at[k, j - 1], xro.at[q, k]
        else:
            ref, send, recv = wxq.at[q, k], xsq.at[k, j - 1], xrq.at[q, k]
        return copy(ref, ref, send, recv, dev)

    def arrived(kind, k, j):
        q = (quarter(k) + j) % 4
        if kind == 0:
            ref, send, recv = wxo.at[core, q, k], xso.at[k, j - 1], xro.at[q, k]
        else:
            ref, send, recv = wxq.at[q, k], xsq.at[k, j - 1], xrq.at[q, k]
        copy(ref, ref, send, recv, (z, sib)).wait_recv()

    def spatial_pair(f, pair):
        off = pl.multiple_of(128 * pair, 128)
        first, second = pair_masks(pair, 128)
        q = qkv_ref[f, :, pl.ds(off, 256)]
        k = qkv_ref[f, :, pl.ds(pl.multiple_of(D + off, 128), 256)]
        v = qkv_ref[f, :, pl.ds(pl.multiple_of(2 * D + off, 128), 256)]
        both = jnp.concatenate([q * first.astype(F32).astype(BF), q * second.astype(F32).astype(BF)], axis=0)
        o = dot(softmax(dot_t(both, k) * SCALE), v)
        rows = slice(128 * f, 128 * f + 128)
        old = sp[rows, pl.ds(off, 256)].astype(F32)
        sp[rows, pl.ds(off, 256)] = jnp.where(first, o[:128], jnp.where(second, o[128:], old)).astype(BF)

    for way in range(2):
        for kind in range(3):
            ring(kind, way, 0, z).start()

    def ring_step(step, _):
        for kinds, f in (((0, 1), 0), ((2,), 1)):
            spatial_pair(f, step)
            for way, steps in ((0, 8), (1, 7)):

                @pl.when(step < steps)
                def _():
                    k = sent(way, step + 1)
                    for kind in kinds:
                        ring(kind, way, step, k).wait_recv()

                    @pl.when(step < steps - 1)
                    def _():
                        for kind in kinds:
                            ring(kind, way, step + 1, k).start()

                    if kinds[0] == 0:
                        for j in range(1, 4):
                            across(0, k, j).start()
                    elif way == 0:
                        for j in range(1, 4):
                            across(2, k, j).start()

        return 0

    lax.fori_loop(0, 8, ring_step, 0)

    def wait_out(i, _):
        for j in range(1, 4):
            arrived(0, (z + i) % NZ, j)
        return 0

    lax.fori_loop(1, NZ, wait_out, 0)
    to_sib = copy(wxo.at[core], wxo.at[core], ls, lr, (z, sib))
    to_sib.start()
    copy(wxo.at[1 - core], wxo.at[1 - core], ls, lr, (z, sib)).wait_recv()

    for t in range(9):
        piece = w8[...] if t == 8 else wxo[t % 2, t // 2]
        wout[:, 128 * t : 128 * t + 128] = piece.astype(F32).reshape(D, 128).astype(BF)
    for low, wide in ((0, 256), (256, 256), (512, 256), (768, 256), (1024, 128)):
        lanes = slice(low, low + wide)
        projected = dot(sp[...], wout[:, lanes])
        res[:, lanes] = (
            hid_ref[:, :, lanes].reshape(256, wide).astype(F32) + mod_ref[0:1, lanes] * projected
        ).astype(BF)

    first_id, second_id = ids_ref[0].astype(F32), ids_ref[1].astype(F32)
    number = jnp.where(iota((BLK, 128), 0) < POS, first_id, second_id).astype(BF)

    def norm(i, _):
        parts = []
        for f in range(2):
            v = res[pl.ds(pl.multiple_of(128 * f + 16 * i, 16), 16), :].astype(F32)
            centred = v - jnp.mean(v, axis=-1, keepdims=True)
            variance = jnp.mean(centred * centred, axis=-1, keepdims=True)
            parts.append(centred * lax.rsqrt(variance + EPS) * (1.0 + mod_ref[2:3, :]) + mod_ref[1:2, :])
        for e in range(2):
            rows = slice(8 * e, 8 * e + 8)
            ns[2 * i + e, :, 0:D] = jnp.concatenate([parts[0][rows], parts[1][rows]], axis=0).astype(BF)
            ns[2 * i + e, :, D:TOK] = number
        return 0

    lax.fori_loop(0, 8, norm, 0)

    def to_owner(j):
        d = (chip + j) % CHIPS
        return copy(ns.at[d], xb.at[1, core, chip], a_s.at[j], a_r.at[chip], (z, d * 2 + core))

    def send_owner(j, _):
        to_owner(j).start()
        return 0

    lax.fori_loop(1, CHIPS, send_owner, 0)
    xb[1, core, chip] = ns[chip]

    def send_rest(i, _):
        for j in range(1, 4):
            across(2, (z + i) % NZ, j).start()
        return 0

    lax.fori_loop(1, 8, send_rest, 0)

    def batch(group, owner, g):
        return xb.at[group, owner, pl.ds(4 * g, 4)]

    def spread(g):
        here = batch(1, core, g)
        return (
            copy(here, batch(0, core, g), hs.at[0, g], hr.at[0, g], (up, seq)),
            copy(here, batch(2, core, g), hs.at[1, g], hr.at[1, g], (down, seq)),
            copy(here, here, ss.at[1, g], sr.at[1, g], (z, sib)),
        )

    def own_batch(g, _):
        for e in range(4):
            d = 4 * g + e

            @pl.when(d != chip)
            def _():
                copy(ns.at[d], xb.at[1, core, d], a_s.at[0], a_r.at[d], (z, sib)).wait_recv()

        for cp in spread(g):
            cp.start()
        return 0

    lax.fori_loop(0, 4, own_batch, 0)

    perm[...] = (frame_order(iota((512, 512), 1)) == iota((512, 512), 0)).astype(F32).astype(BF)
    perm_t[...] = (frame_order(iota((512, 512), 0)) == iota((512, 512), 1)).astype(F32).astype(BF)

    def wait_qkv(i, _):
        for j in range(1, 4):
            arrived(2, (z + i) % NZ, j)
        return 0

    lax.fori_loop(1, NZ, wait_qkv, 0)
    for q in range(4):
        for u in range(4):
            lanes = slice(128 * u, 128 * u + 128)
            wqkv[:, 512 * q + 128 * u : 512 * q + 128 * u + 128] = (
                wxq[q, :, :, lanes].astype(F32).reshape(D, 128).astype(BF)
            )

    def from_sib(group, g):
        there = batch(group, 1 - core, g)
        return copy(there, there, ss.at[group, g], sr.at[group, g], (z, sib))

    def sort_group(group):
        rows = xb[group].reshape(512, TOK)

        xp[group] = dot(perm[...], rows).astype(BF)

    def keys_values(group):
        def chunk(n, _):
            lanes = pl.ds(pl.multiple_of(256 * n, 128), 256)
            from_lanes = pl.ds(pl.multiple_of(HALF + 256 * n, 128), 256)
            made = dot(xp[group, :, 0:D], wqkv[:, from_lanes]).astype(BF)
            kv[:, 64 * group : 64 * group + 64, lanes] = made.reshape(POS, 64, 256)
            return 0

        lax.fori_loop(0, 5, chunk, 0)

    def wait_sib(group):
        for g in range(4):
            from_sib(group, g).wait_recv()

    wait_sib(1)
    sort_group(1)
    for low, wide in ((0, 256), (256, 256), (512, 128)):
        qs[:, low : low + wide] = dot(xp[1, :, 0:D], wqkv[:, low : low + wide]).astype(BF)
    keys_values(1)

    def relay(way, group, g):
        got = batch(group, core, g)
        return copy(got, got, ss.at[group, g], sr.at[group, g], (z, sib))

    for g in range(4):
        for way, group in ((0, 0), (1, 2)):
            got = batch(group, core, g)
            copy(got, got, hs.at[way, g], hr.at[way, g], (z, sib)).wait_recv()
            relay(way, group, g).start()
    for group in (0, 2):
        wait_sib(group)
        sort_group(group)
        keys_values(group)

    lane = iota((64, 128), 1)
    ids_q = xp[1, 0:64, D:TOK].astype(F32)
    ids_k = jnp.concatenate([xp[g, 0:64, D:TOK] for g in range(3)], axis=0).astype(F32)
    left = jnp.where(lane == 0, ids_q, jnp.where(lane == 1, 1.0, 0.0)).astype(BF)
    lane3 = iota((192, 128), 1)
    right = jnp.where(lane3 == 0, 1.0, jnp.where(lane3 == 1, -ids_k, 0.0)).astype(BF)
    apart = dot_t(left, right)
    same = jnp.concatenate([apart, apart], axis=0) == 0.0

    def position(p, _):
        rows = pl.ds(pl.multiple_of(64 * p, 64), 64)
        made = []
        for i in range(4):
            first, second = pair_masks(4 * core + i, 64)
            lanes = slice(128 * i, 128 * i + 256)
            q = qs[rows, lanes]
            k = kv[p, :, lanes]
            v = kv[p, :, HALF + 128 * i : HALF + 128 * i + 256]
            both = jnp.concatenate([q * first.astype(F32).astype(BF), q * second.astype(F32).astype(BF)], axis=0)
            scores = jnp.where(same, dot_t(both, k) * SCALE, NEG)
            o = dot(softmax(scores), v)
            made.append(jnp.where(first, o[:64], jnp.where(second, o[64:], 0.0)))
        tiles = [made[0][:, :128]]
        for i in range(1, 4):
            tiles.append(made[i - 1][:, 128:] + made[i][:, :128])
        tiles.append(made[3][:, 128:])
        for u in range(5):
            tt[rows, 128 * u : 128 * u + 128] = tiles[u].astype(BF)
        return 0

    lax.fori_loop(0, POS, position, 0)

    tb[...] = dot(perm_t[...], tt[...]).astype(BF).reshape(2, CHIPS, BLK, HALF)

    def to_frames(j):
        d = (seq + j) % 32
        return copy(tb.at[d % 2, d // 2], rb.at[core, chip], r_s.at[j], r_r.at[seq], (z, d))

    def send_back(j, _):
        to_frames(j).start()
        return 0

    lax.fori_loop(1, 32, send_back, 0)
    rb[core, chip] = tb[core, chip]

    def wait_back(j, _):
        d = (seq + j) % 32
        copy(tb.at[0, 0], rb.at[d % 2, d // 2], r_s.at[0], r_r.at[d], (z, sib)).wait_recv()
        return 0

    lax.fori_loop(1, 32, wait_back, 0)

    def finish(i, _):
        whole = []
        for e in range(2):
            a, b = rb[0, 2 * i + e].astype(F32), rb[1, 2 * i + e].astype(F32)
            whole.append(jnp.concatenate([a[:, :512], a[:, 512:] + b[:, :128], b[:, 128:]], axis=1))
        for f in range(2):
            rows = slice(8 * f, 8 * f + 8)
            temporal = jnp.concatenate([whole[0][rows], whole[1][rows]], axis=0)
            at = pl.multiple_of(16 * i, 16)
            kept = res[pl.ds(pl.multiple_of(128 * f + 16 * i, 16), 16), :].astype(F32)
            out_ref[f, pl.ds(at, 16), :] = (kept + mod_ref[3:4, :] * temporal).astype(BF)
        return 0

    lax.fori_loop(0, 8, finish, 0)

    for way, steps in ((0, 8), (1, 7)):
        for kind in range(3):

            def drain_ring(step, _):
                ring(kind, way, step, sent(way, step)).wait_send()
                return 0

            lax.fori_loop(0, steps, drain_ring, 0)

    def drain_across(i, _):
        for j in range(1, 4):
            across(0, (z + i) % NZ, j).wait_send()
            across(2, (z + i) % NZ, j).wait_send()
        return 0

    lax.fori_loop(1, NZ, drain_across, 0)
    to_sib.wait_send()

    def drain_owner(j, _):
        to_owner(j).wait_send()
        return 0

    lax.fori_loop(1, CHIPS, drain_owner, 0)

    def drain_batch(g, _):
        for cp in spread(g):
            cp.wait_send()
        relay(0, 0, g).wait_send()
        relay(1, 2, g).wait_send()
        return 0

    lax.fori_loop(0, 4, drain_batch, 0)

    def drain_back(j, _):
        to_frames(j).wait_send()
        return 0

    lax.fori_loop(1, 32, drain_back, 0)


def shards(hidden_states, spatial_qkv, spatial_out_weight, temporal_qkv_weight, modulation, video_ids):
    vmem = pl.BlockSpec(memory_space=pltpu.VMEM)
    dma = pltpu.SemaphoreType.DMA
    return pl.pallas_call(
        kernel,
        out_shape=jax.ShapeDtypeStruct(hidden_states.shape, BF),
        in_specs=[vmem] * 5 + [pl.BlockSpec(memory_space=pltpu.SMEM)],
        out_specs=vmem,
        scratch_shapes=[
            pltpu.VMEM((NZ, ROWS, 128), BF),
            pltpu.VMEM((2, 4, NZ, ROWS, 128), BF),
            pltpu.VMEM((4, NZ, ROWS, 512), BF),
            pltpu.VMEM((D, D), BF),
            pltpu.VMEM((D, 2048), BF),
            pltpu.VMEM((256, D), BF),
            pltpu.VMEM((256, D), BF),
            pltpu.VMEM((CHIPS, BLK, TOK), BF),
            pltpu.VMEM((3, 2, CHIPS, BLK, TOK), BF),
            pltpu.VMEM((3, 512, TOK), BF),
            pltpu.VMEM((512, HALF), BF),
            pltpu.VMEM((POS, 192, 2 * HALF), BF),
            pltpu.VMEM((512, HALF), BF),
            pltpu.VMEM((2, CHIPS, BLK, HALF), BF),
            pltpu.VMEM((2, CHIPS, BLK, HALF), BF),
            pltpu.VMEM((512, 512), BF),
            pltpu.VMEM((512, 512), BF),
            dma((2, 3, 8)),
            dma((2, 3, 8)),
            dma((NZ, 3)),
            dma((4, NZ)),
            dma((NZ, 3)),
            dma((4, NZ)),
            dma,
            dma,
            dma((CHIPS,)),
            dma((CHIPS,)),
            dma((2, 4)),
            dma((2, 4)),
            dma((3, 4)),
            dma((3, 4)),
            dma((32,)),
            dma((32,)),
        ],
        compiler_params=pltpu.CompilerParams(
            collective_id=0, has_side_effects=True, vmem_limit_bytes=58 * 2**20
        ),
        cost_estimate=pl.CostEstimate(flops=7_000_000_000, bytes_accessed=5_000_000, transcendentals=2_000_000),
    )(hidden_states, spatial_qkv, spatial_out_weight, temporal_qkv_weight, modulation, video_ids)


def solution(mesh):
    in_specs = (
        P(("dp", "seq"), None, None),
        P(("dp", "seq"), None, None),
        P("dp", None),
        P("dp", None),
        P(),
        P(("dp", "seq")),
    )
    out_specs = P(("dp", "seq"), None, None)
    return jax.shard_map(shards, mesh=mesh, in_specs=in_specs, out_specs=out_specs, check_vma=False)
```

time: 315 us -> 120 us (0.38)
  waiting for transfers between devices: 183 us -> 0 us
  Pallas kernels: 0 us -> 118 us
  blocking collectives: 59.4 us -> 0 us
  local copies, waits for them, and re-layouts: 26 us -> 1.92 us
  matrix products: 15.6 us -> 0 us
  between operations: 14.3 us -> 0.01 us
  starting transfers between devices: 9.1 us -> 0 us
  other arithmetic: 7.82 us -> 0 us
    all_gather x2 -> x0, waiting for transfers between devices: 171 us -> none  [the longest x1 106 us: shards(): lax.all_gather(temporal_qkv_weight, 'dp', axis=0, tiled=True)]
    pallas_call x0 -> x1, Pallas kernels: none -> 118 us  [shards(): pl.pallas_call(kernel, out_shape=jax.ShapeDtypeStruct(hidden_states.shape...]
    all_to_all x2 -> x0, blocking collectives: 48.4 us -> none  [the longest x1 32.2 us: shards(): lax.all_to_all(local_qkv, 'seq', split_axis=1, concat_axis=0, tiled=True)]
    dot_general x5 -> x0, matrix products: 13.4 us -> none  [the longest x2 8.84 us: add_rows(): return jnp.dot(left, piece, preferred_element_type=jnp.float32)]
    slice x5 -> x0, local copies, waits for them, and re-layouts: 13.3 us -> none  [the longest x2 6.78 us: shards(): keyvals[:, :, :width].reshape(3 * group_frames, local_patches, HEADS, HD)]
    unnamed x1 -> x0, blocking collectives: 11 us -> none
    ppermute x4 -> x0, waiting for transfers between devices: 10 us -> none  [the longest x2 5.12 us: with_halo(): lax.ppermute(lax.slice_in_dim(block, block.shape[dim] - width, None, axis...]
    ppermute x4 -> x0, starting transfers between devices: 9.06 us -> none  [the longest x2 6.31 us: with_halo(): lax.ppermute(lax.slice_in_dim(block, block.shape[dim] - width, None, axis...]
  transfers between devices with their start and end apart: 6 -> 0, of which waited for: 4 -> 0; matrix products, arithmetic and copies ran while one was open for 5% -> 0% of each run, Pallas kernels for 0% -> 0%
where the time goes in v1:
time: 120 us
  Pallas kernels  118 us (98%)
  local copies, waits for them, and re-layouts  1.92 us (2%)
    pallas_call x1, Pallas kernels, shards(): pl.pallas_call(kernel, out_shape=jax.ShapeDtypeStruct(hidden_states.shape...  118 us

profile of v1, /device:TPU:1, one launch (start us, length us, event | category | flops | bytes accessed | tf_op | source)
XLA Modules:
  0.0 119.8 jit_solution(7516972485895831676)
XLA Ops:
  0.0 117.8 %shard_map.64 = bf16[2,128,1152]{2,1,0:T(8,128)(2,1)} custom-call(bf16[2,128,1152]{2,1,0:T(8,128)(2,1)} %hid_ref.1, bf16[2,128,3456]{2,1,0:T(8,128)(2,1)} %qkv_ref.1, bf16[72,1152]{1,0:T(8,128)(2,1)} %wo_ref.1, bf16[72,3456]{1,0:T(8,128)(2,1)} %wt_ref.1, f32[4,1152]{1,0:T(4,128)} %mod_ref.1, s32[2]{0:T(128)} %ids_ref.1), custom_call_target="tpu_custom_call" | custom-call | flops 7000000000 | bytes 5000000 | tf_op jit(solution)/shard_map/pallas_call | solution.py:418
  117.8 1.9 %copy.8 = bf16[2,128,1152]{2,1,0:T(8,128)(2,1)} copy(bf16[2,128,1152]{2,1,0:T(8,128)(2,1)} %shard_map.64) | data formatting | bytes 1179648

commit v2 on v1

v2 whole, which is shorter than its diff:
```python
import math

import jax
import jax.numpy as jnp
from jax import lax
from jax.experimental import pallas as pl
from jax.experimental.pallas import tpu as pltpu
from jax.sharding import PartitionSpec as P

HEADS = 16
HD = 72
D = 1152
NEG = -1e30
EPS = 1e-06
SCALE = 1.0 / math.sqrt(HD)

NZ = 16
ROWS = 72
CHIPS = 16
POS = 8
BLK = 16
TOK = 1280
HALF = 640
PARTS = ((0, 256), (256, 384))
MESH = pl.DeviceIdType.MESH
BF = jnp.bfloat16
F32 = jnp.float32


def iota(shape, dim):
    return lax.broadcasted_iota(jnp.int32, shape, dim)


def dot(a, b):
    return jnp.dot(a, b, preferred_element_type=F32)


def dot_t(a, b):
    return lax.dot_general(a, b, (((1,), (1,)), ((), ())), preferred_element_type=F32)


def softmax(scores):
    top = jnp.max(scores, axis=-1, keepdims=True)
    powers = jnp.exp(scores - top)
    return (powers * (1.0 / jnp.sum(powers, axis=-1, keepdims=True))).astype(BF)


def pair_masks(pair, rows):
    lane = iota((rows, 256), 1)
    low = 16 * pair
    first = (lane >= low) & (lane < low + HD)
    second = (lane >= low + HD) & (lane < low + 2 * HD)
    return first, second


def sorted_place(rows):
    chip, two, pos = rows // 16, (rows % 16) // 8, rows % 8
    return pos * 8 + chip * 2 + two


def by_position(rows, p):
    return jnp.concatenate([rows[64 * b + 8 * p : 64 * b + 8 * p + 8] for b in range(rows.shape[0] // 64)], axis=0)


def kernel(
    hid_ref, qkv_ref, wo_ref, wt_ref, mod_ref, ids_ref, out_ref,
    w8, wxo, wxq, wout, wqkv, sp, res, ns, xa, xs, qs, kt, vs, tt, carry, tba, tbb, rba, rbb,
    zs, zr, xsq, xrq, zso, zro, xso, xro, zs8, zr8, xs8, xr8, ls, lr, a_s, a_r, hs, hr, ss, sr, r_s, r_r,
):
    z, seq = lax.axis_index("dp"), lax.axis_index("seq")
    core, chip = seq % 2, seq // 2
    x, y = chip // 4, chip % 4
    up, down, sib = (z + 1) % NZ, (z + NZ - 1) % NZ, chip * 2 + (1 - core)

    def copy(src, dst, send, recv, dev):
        return pltpu.make_async_remote_copy(
            src_ref=src, dst_ref=dst, send_sem=send, recv_sem=recv, device_id=dev, device_id_type=MESH
        )

    barrier = pltpu.get_barrier_semaphore()

    def greet(j, _):
        pl.semaphore_signal(barrier, inc=1, device_id=(z, (seq + j) % 32), device_id_type=MESH)
        return 0

    lax.fori_loop(1, 32, greet, 0)
    for dz in (1, 2, 4, 8, 12, 14, 15):
        pl.semaphore_signal(barrier, inc=1, device_id=((z + dz) % NZ, seq), device_id_type=MESH)

    for q in range(4):
        wxo[core, q, z] = wo_ref[:, pl.ds(pl.multiple_of(256 * q + 128 * core, 128), 128)]
        for u in range(4):
            n = min(4 * q + u, 14)
            lanes = pl.ds(pl.multiple_of((n // 5) * D + 128 * (n % 5) + 512 * core, 128), 128)
            wxq[q, z, :, 128 * u : 128 * u + 128] = wt_ref[:, lanes]

    @pl.when(z // 8 == core)
    def _():
        w8[z] = wo_ref[:, 1024:1152]

    sp[...] = jnp.zeros_like(sp)
    pl.semaphore_wait(barrier, 38)

    def quarter(k):
        odd = (k // 2) % 2
        return y * (1 - odd) + x * odd

    def has_last(k):
        return (quarter(k) == (k // 2) % 4) & (k // 8 == core)

    def ring(way, k):
        ref = wxq.at[quarter(k), k]
        return copy(ref, ref, zs, zr.at[k], (up, seq) if way == 0 else (down, seq))

    def sent(way, step):
        return (z + NZ - step) % NZ if way == 0 else (z + step) % NZ

    def neighbour(k, j):
        odd = (k // 2) % 2
        return (z, (((x + j * odd) % 4) * 4 + (y + j * (1 - odd)) % 4) * 2 + core)

    def across(k, j):
        ref = wxq.at[quarter(k), k]
        ahead = k % 2 if j == 1 else 1 - k % 2
        return copy(ref, ref, xsq, xrq.at[k * ahead + NZ * (1 - ahead)], neighbour(k, j))

    def hand_on(k):
        j = 3 - 2 * (k % 2)
        ref = wxq.at[(quarter(k) + 4 - j) % 4, k]
        copy(ref, ref, xsq, xrq.at[k], neighbour(k, j)).wait_recv()
        copy(ref, ref, xsq, xrq.at[NZ], neighbour(k, j)).start()

    def out_along(k, dz):
        ref = wxo.at[core, quarter(k), k]
        return copy(ref, ref, zso, zro.at[k], ((z + dz + NZ) % NZ, seq))

    def out_across(k, j):
        ref = wxo.at[core, quarter(k), k]
        return copy(ref, ref, xso, xro, neighbour(k, j))

    def last_along(k, dz):
        return copy(w8.at[k], w8.at[k], zs8, zr8.at[k], ((z + dz + NZ) % NZ, seq))

    def last_across(k, j):
        return copy(w8.at[k], w8.at[k], xs8, xr8.at[k], neighbour(k, j))

    def near(k):
        return (1, -1, 2 - 4 * ((k // 4) % 2))

    def send_near(k):
        for dz in near(k):
            out_along(k, dz).start()

        @pl.when(has_last(k))
        def _():
            for dz in near(k):
                last_along(k, dz).start()

    def send_across(k):
        for j in range(1, 4):
            out_across(k, j).start()

        @pl.when(has_last(k))
        def _():
            for j in range(1, 4):
                last_across(k, j).start()

    def wait_along(k):
        out_along(k, 1).wait_recv()

        @pl.when(has_last(k))
        def _():
            last_along(k, 1).wait_recv()

    def spatial_pair(f, pair):
        off = pl.multiple_of(128 * pair, 128)
        first, second = pair_masks(pair, 128)
        q = qkv_ref[f, :, pl.ds(off, 256)]
        k = qkv_ref[f, :, pl.ds(pl.multiple_of(D + off, 128), 256)]
        v = qkv_ref[f, :, pl.ds(pl.multiple_of(2 * D + off, 128), 256)]
        both = jnp.concatenate([q * first.astype(F32).astype(BF), q * second.astype(F32).astype(BF)], axis=0)
        o = dot(softmax(dot_t(both, k) * SCALE), v)
        rows = slice(128 * f, 128 * f + 128)
        old = sp[rows, pl.ds(off, 256)].astype(F32)
        sp[rows, pl.ds(off, 256)] = jnp.where(first, o[:128], jnp.where(second, o[128:], old)).astype(BF)

    def spatial_pairs(low, high):
        def one(i, _):
            for f in range(2):
                spatial_pair(f, i)
            return 0

        lax.fori_loop(low, high, one, 0)

    def ring_step(distance):
        for way in range(2 if distance < 8 else 1):
            k = sent(way, distance)
            ring(way, k).wait_recv()
            if distance not in (3, 7 + way, 8):
                ring(way, k).start()

    def ring_across(*distances):
        for j in (1, 3):
            for distance in distances:
                for way in range(2 if distance < 8 else 1):
                    across(sent(way, distance), j).start()

    def ring_hand_on(distance):
        for way in range(2 if distance < 8 else 1):
            hand_on(sent(way, distance))

    for dz in (8, 4, -4):
        out_along(z, dz).start()

    @pl.when(has_last(z))
    def _():
        for dz in (8, 4, -4):
            last_along(z, dz).start()

    send_near(z)
    for way in range(2):
        ring(way, z).start()

    for dz in (4, -4):
        ref = wxq.at[quarter(z), z]
        copy(ref, ref, zs, zr.at[z], ((z + dz + NZ) % NZ, seq)).start()
    spatial_pairs(0, 2)

    def far(i, _):
        k = (z + 4 + 8 * i - 12 * (i // 2)) % NZ
        wait_along(k)
        send_near(k)
        send_across(k)
        return 0

    lax.fori_loop(0, 3, far, 0)
    ring_step(1)
    ring_across(1)
    spatial_pairs(2, 6)

    def rest(i, _):
        k = (z + 4 * (i % 4) + 1 + i // 4) % NZ
        wait_along(k)
        send_across(k)
        return 0

    lax.fori_loop(0, 8, rest, 0)
    ring_step(4)
    ring_across(4)
    lax.fori_loop(8, 12, rest, 0)
    ring_step(2)
    ring_across(2)
    ring_hand_on(1)
    ring_step(5)
    ring_across(5)
    ring_step(3)
    ring_across(3)
    ring_hand_on(4)

    def wait_last(k, _):
        @pl.when((k != z) & (k // 8 == core) & (quarter(k) != (k // 2) % 4))
        def _():
            last_across(k, 1).wait_recv()

        return 0

    lax.fori_loop(0, NZ, wait_last, 0)
    pieces = wxo.at[core, pl.ds(0, 3), pl.ds(0, NZ - 1)]
    copy(pieces, pieces, xso, xro, (z, sib)).wait_recv()
    to_sib = copy(wxo.at[core], wxo.at[core], ls.at[0], lr.at[0], (z, sib))
    to_sib.start()
    mine, other = w8.at[pl.ds(8 * core, 8)], w8.at[pl.ds(8 * (1 - core), 8)]
    last_to_sib = copy(mine, mine, ls.at[1], lr.at[1], (z, sib))
    last_to_sib.start()
    spatial_pairs(6, 7)
    ring_step(6)
    ring_across(6)
    ring_hand_on(2)
    spatial_pairs(7, 8)
    copy(wxo.at[1 - core], wxo.at[1 - core], ls.at[0], lr.at[0], (z, sib)).wait_recv()
    copy(other, other, ls.at[1], lr.at[1], (z, sib)).wait_recv()

    for t in range(9):
        piece = w8[...] if t == 8 else wxo[t % 2, t // 2]
        wout[:, 128 * t : 128 * t + 128] = piece.astype(F32).reshape(D, 128).astype(BF)
    for low, wide in ((0, 256), (256, 256), (512, 256), (768, 256), (1024, 128)):
        lanes = slice(low, low + wide)
        projected = dot(sp[...], wout[:, lanes])
        res[:, lanes] = (
            hid_ref[:, :, lanes].reshape(256, wide).astype(F32) + mod_ref[0:1, lanes] * projected
        ).astype(BF)

    def to_owner(d):
        return copy(ns.at[d], xa.at[chip], a_s, a_r.at[chip // 4], (z, d * 2 + core))

    first_id, second_id = ids_ref[0].astype(F32), ids_ref[1].astype(F32)
    number = jnp.where(iota((BLK, 128), 0) < POS, first_id, second_id).astype(BF)

    def norm(step, _):
        i = (step + chip // 2) % 8
        parts = []
        for f in range(2):
            v = res[pl.ds(pl.multiple_of(128 * f + 16 * i, 16), 16), :].astype(F32)
            centred = v - jnp.mean(v, axis=-1, keepdims=True)
            variance = jnp.mean(centred * centred, axis=-1, keepdims=True)
            parts.append(centred * lax.rsqrt(variance + EPS) * (1.0 + mod_ref[2:3, :]) + mod_ref[1:2, :])
        for e in range(2):
            rows = slice(8 * e, 8 * e + 8)
            ns[2 * i + e, :, 0:D] = jnp.concatenate([parts[0][rows], parts[1][rows]], axis=0).astype(BF)
            ns[2 * i + e, :, D:TOK] = number

            @pl.when(2 * i + e != chip)
            def _():
                to_owner(2 * i + e).start()

        return 0

    lax.fori_loop(0, 8, norm, 0)

    xa[chip] = ns[chip]
    sort = (sorted_place(iota((64, 64), 1)) == iota((64, 64), 0)).astype(F32).astype(BF)
    unsort = (sorted_place(iota((64, 64), 0)) == iota((64, 64), 1)).astype(F32).astype(BF)
    ring_step(7)
    ring_across(7)
    ring_hand_on(5)

    def batch(group, owner, g):
        return xs.at[group, owner, g]

    def spread(g):
        here = batch(1, core, g)
        copy(here, batch(0, core, g), hs, hr.at[0, g], (up, seq)).start()
        copy(here, batch(2, core, g), hs, hr.at[1, g], (down, seq)).start()
        copy(here, here, ss, sr.at[1, g], (z, sib)).start()

    def own_batch(g):
        @pl.when(chip // 4 == g)
        def _():
            three = ns.at[pl.ds(0, 3)]
            copy(three, three, a_s, a_r.at[g], (z, sib)).wait_recv()

        @pl.when(chip // 4 != g)
        def _():
            four = ns.at[pl.ds(0, 4)]
            copy(four, four, a_s, a_r.at[g], (z, sib)).wait_recv()

        xs[1, core, g] = dot(sort, xa[pl.ds(4 * g, 4)].reshape(64, TOK)).astype(BF)
        spread(g)

    own_batch(0)
    ring_hand_on(3)
    own_batch(1)
    ring_step(8)
    ring_across(8)
    own_batch(2)
    ring_hand_on(6)
    own_batch(3)
    ring_hand_on(7)
    ring_hand_on(8)

    pieces = wxq.at[pl.ds(0, 2), pl.ds(0, NZ - 1)]
    copy(pieces, pieces, xsq, xrq.at[NZ], (z, sib)).wait_recv()
    for q in range(4):
        for u in range(4):
            lanes = slice(128 * u, 128 * u + 128)
            wqkv[:, 512 * q + 128 * u : 512 * q + 128 * u + 128] = (
                wxq[q, :, :, lanes].astype(F32).reshape(D, 128).astype(BF)
            )

    def wait_sib(group):
        for g in range(4):
            there = batch(group, 1 - core, g)
            copy(there, there, ss, sr.at[group, g], (z, sib)).wait_recv()

    def project(groups, low, wide):
        rows = [xs[group, :, :, :, 0:D].reshape(512, D) for group in groups]
        return dot(jnp.concatenate(rows, axis=0) if len(rows) > 1 else rows[0], wqkv[:, low : low + wide])

    def keys_values(groups, first_key):
        keys = slice(first_key, first_key + 64 * len(groups))
        for low, wide in ((0, 256), (256, 256), (512, 128)):
            made = project(groups, HALF + low, wide)
            for p in range(POS):
                kt[p, low : low + wide, keys] = by_position(made, p).T.astype(BF)
            made = project(groups, 2 * HALF + low, wide)
            for p in range(POS):
                vs[p, keys, low : low + wide] = by_position(made, p).astype(BF)

    wait_sib(1)
    for low, wide in ((0, 256), (256, 256), (512, 128)):
        made = project((1,), low, wide)
        for p in range(POS):
            qs[64 * p : 64 * p + 64, low : low + wide] = by_position(made, p).astype(BF)
    keys_values((1,), 128)

    def relay(group, g):
        got = batch(group, core, g)
        return copy(got, got, ss, sr.at[group, g], (z, sib))

    for g in range(4):
        for way, group in ((0, 0), (1, 2)):
            got = batch(group, core, g)
            copy(got, got, hs, hr.at[way, g], (z, sib)).wait_recv()
            relay(group, g).start()
    for group in (0, 2):
        wait_sib(group)
    keys_values((0, 2), 0)

    lane = iota((64, 128), 1)
    def ids_of(group):
        first = xs[group, :, :, 0:16, D:TOK].astype(F32)
        return jnp.concatenate([first[b // 4, b % 4, 0:8] for b in range(8)], axis=0)

    ids_q = ids_of(1)
    ids_k = jnp.concatenate([ids_of(0), ids_of(2), ids_q], axis=0)
    left = jnp.where(lane == 0, ids_q, jnp.where(lane == 1, 1.0, 0.0)).astype(BF)
    lane3 = iota((192, 128), 1)
    right = jnp.where(lane3 == 0, 1.0, jnp.where(lane3 == 1, -ids_k, 0.0)).astype(BF)
    apart = dot_t(left, right)
    same = jnp.concatenate([apart, apart], axis=0) == 0.0

    def send_back(part, made):
        low, wide = PARTS[part]
        for b in range(8):
            rows = dot(unsort, tt[b, :, low : low + wide].astype(BF)).astype(BF)
            made[4 * b : 4 * b + 4] = rows.reshape(4, BLK, wide)

        def one(j, _):
            d = (seq + j) % 32
            from_ref, to_ref = made.at[(d % 2) * CHIPS + d // 2], (rba, rbb)[part].at[core * CHIPS + chip]
            copy(from_ref, to_ref, r_s.at[part], r_r.at[part], (z, d)).start()
            return 0

        lax.fori_loop(1, 32, one, 0)
        (rba, rbb)[part][core * CHIPS + chip] = made[core * CHIPS + chip]

    for i in range(4):
        first, second = pair_masks(4 * core + i, 64)
        first_one, second_one = first.astype(F32).astype(BF), second.astype(F32).astype(BF)
        lanes = slice(128 * i, 128 * i + 256)

        def positions(step, _):
            for e in range(4):
                p = 4 * step + e
                rows = pl.ds(pl.multiple_of(64 * p, 64), 64)
                q = qs[rows, lanes]
                both = jnp.concatenate([q * first_one, q * second_one], axis=0)
                scores = jnp.where(same, dot(both, kt[p, lanes, :]) * SCALE, NEG)
                o = dot(softmax(scores), vs[p, :, lanes])
                made = jnp.where(first, o[:64], jnp.where(second, o[64:], 0.0))
                low = made[:, :128]
                if i > 0:
                    low = low + carry[rows, :]
                to = pl.ds(pl.multiple_of(8 * p, 8), 8)
                for b in range(8):
                    tt[b, to, 128 * i : 128 * i + 128] = low[8 * b : 8 * b + 8]
                    if i == 3:
                        tt[b, to, 512:640] = made[8 * b : 8 * b + 8, 128:]
                if i < 3:
                    carry[rows, :] = made[:, 128:]
            return 0

        lax.fori_loop(0, POS // 4, positions, 0)
        if i == 1:
            send_back(0, tba)

    send_back(1, tbb)
    for part, ref in ((0, rba), (1, rbb)):
        others = ref.at[pl.ds(0, 31)]
        copy(others, others, r_s.at[part], r_r.at[part], (z, sib)).wait_recv()

    def finish(i, _):
        whole = []
        for e in range(2):
            here, there = 2 * i + e, CHIPS + 2 * i + e
            low, low2 = rba[here].astype(F32), rba[there].astype(F32)
            high, high2 = rbb[here].astype(F32), rbb[there].astype(F32)
            whole.append(
                jnp.concatenate([low, high[:, :256], high[:, 256:] + low2[:, :128], low2[:, 128:], high2], axis=1)
            )
        for f in range(2):
            rows = slice(8 * f, 8 * f + 8)
            temporal = jnp.concatenate([whole[0][rows], whole[1][rows]], axis=0)
            at = pl.multiple_of(16 * i, 16)
            kept = res[pl.ds(pl.multiple_of(128 * f + 16 * i, 16), 16), :].astype(F32)
            out_ref[f, pl.ds(at, 16), :] = (kept + mod_ref[3:4, :] * temporal).astype(BF)
        return 0

    lax.fori_loop(0, 8, finish, 0)

    def drain(ref, sem):
        copy(ref, ref, sem, lr.at[0], (z, sib)).wait_send()

    drain(wxq.at[0, pl.ds(0, 15)], zs)
    drain(wxq.at[pl.ds(0, 3), pl.ds(0, 15)], xsq)
    drain(wxo.at[0, 0, pl.ds(0, 15)], zso)
    drain(wxo.at[0, pl.ds(0, 3), pl.ds(0, 15)], xso)

    def drain_last(k, _):
        @pl.when(has_last(k))
        def _():
            @pl.when((k - z + NZ) % 4 == 0)
            def _():
                drain(w8.at[pl.ds(0, 3)], zs8)

            @pl.when(k == z)
            def _():
                drain(w8.at[pl.ds(0, 3)], zs8)

            @pl.when(k != z)
            def _():
                drain(w8.at[pl.ds(0, 3)], xs8)

        return 0

    lax.fori_loop(0, NZ, drain_last, 0)
    to_sib.wait_send()
    last_to_sib.wait_send()
    drain(ns.at[pl.ds(0, 15)], a_s)
    drain(xs.at[0], hs)
    drain(xs.at[pl.ds(0, 3), 0], ss)
    drain(rba.at[pl.ds(0, 31)], r_s.at[0])
    drain(rbb.at[pl.ds(0, 31)], r_s.at[1])


def shards(hidden_states, spatial_qkv, spatial_out_weight, temporal_qkv_weight, modulation, video_ids):
    vmem = pl.BlockSpec(memory_space=pltpu.VMEM)
    dma = pltpu.SemaphoreType.DMA
    return pl.pallas_call(
        kernel,
        out_shape=jax.ShapeDtypeStruct(hidden_states.shape, BF),
        in_specs=[vmem] * 5 + [pl.BlockSpec(memory_space=pltpu.SMEM)],
        out_specs=vmem,
        scratch_shapes=[
            pltpu.VMEM((NZ, ROWS, 128), BF),
            pltpu.VMEM((2, 4, NZ, ROWS, 128), BF),
            pltpu.VMEM((4, NZ, ROWS, 512), BF),
            pltpu.VMEM((D, D), BF),
            pltpu.VMEM((D, 2048), BF),
            pltpu.VMEM((256, D), BF),
            pltpu.VMEM((256, D), BF),
            pltpu.VMEM((CHIPS, BLK, TOK), BF),
            pltpu.VMEM((CHIPS, BLK, TOK), BF),
            pltpu.VMEM((3, 2, 4, 64, TOK), BF),
            pltpu.VMEM((512, HALF), BF),
            pltpu.VMEM((POS, HALF, 192), BF),
            pltpu.VMEM((POS, 192, HALF), BF),
            pltpu.VMEM((8, 64, HALF), F32),
            pltpu.VMEM((512, 128), F32),
            pltpu.VMEM((32, BLK, 256), BF),
            pltpu.VMEM((32, BLK, 384), BF),
            pltpu.VMEM((32, BLK, 256), BF),
            pltpu.VMEM((32, BLK, 384), BF),
            dma,
            dma((NZ,)),
            dma,
            dma((NZ + 1,)),
            dma,
            dma((NZ,)),
            dma,
            dma,
            dma,
            dma((NZ,)),
            dma,
            dma((NZ,)),
            dma((2,)),
            dma((2,)),
            dma,
            dma((4,)),
            dma,
            dma((2, 4)),
            dma,
            dma((3, 4)),
            dma((2,)),
            dma((2,)),
        ],
        compiler_params=pltpu.CompilerParams(
            collective_id=0, has_side_effects=True, vmem_limit_bytes=58 * 2**20
        ),
        cost_estimate=pl.CostEstimate(flops=7_000_000_000, bytes_accessed=5_000_000, transcendentals=2_000_000),
    )(hidden_states, spatial_qkv, spatial_out_weight, temporal_qkv_weight, modulation, video_ids)


def solution(mesh):
    in_specs = (
        P(("dp", "seq"), None, None),
        P(("dp", "seq"), None, None),
        P("dp", None),
        P("dp", None),
        P(),
        P(("dp", "seq")),
    )
    out_specs = P(("dp", "seq"), None, None)
    return jax.shard_map(shards, mesh=mesh, in_specs=in_specs, out_specs=out_specs, check_vma=False)
```

time: 120 us -> 105 us (0.88)
  Pallas kernels: 118 us -> 103 us
    pallas_call x1, Pallas kernels: 118 us -> 103 us  [shards(): pl.pallas_call(kernel, out_shape=jax.ShapeDtypeStruct(hidden_states.shape...]
where the time goes in v2:
time: 105 us
  Pallas kernels  103 us (98%)
  local copies, waits for them, and re-layouts  1.92 us (2%)
    pallas_call x1, Pallas kernels, shards(): pl.pallas_call(kernel, out_shape=jax.ShapeDtypeStruct(hidden_states.shape...  103 us

profile of v2, /device:TPU:1, one launch (start us, length us, event | category | flops | bytes accessed | tf_op | source)
XLA Modules:
  0.0 104.9 jit_solution(18036206637077225108)
XLA Ops:
  0.0 103.0 %shard_map.64 = bf16[2,128,1152]{2,1,0:T(8,128)(2,1)} custom-call(bf16[2,128,1152]{2,1,0:T(8,128)(2,1)} %hid_ref.1, bf16[2,128,3456]{2,1,0:T(8,128)(2,1)} %qkv_ref.1, bf16[72,1152]{1,0:T(8,128)(2,1)} %wo_ref.1, bf16[72,3456]{1,0:T(8,128)(2,1)} %wt_ref.1, f32[4,1152]{1,0:T(4,128)} %mod_ref.1, s32[2]{0:T(128)} %ids_ref.1), custom_call_target="tpu_custom_call" | custom-call | flops 7000000000 | bytes 5000000 | tf_op jit(solution)/shard_map/pallas_call | solution.py:529
  103.0 1.9 %copy.8 = bf16[2,128,1152]{2,1,0:T(8,128)(2,1)} copy(bf16[2,128,1152]{2,1,0:T(8,128)(2,1)} %shard_map.64) | data formatting | bytes 1179648

commit v3 on v2

--- a/solution.py
+++ b/solution.py
@@ -13,13 +13,13 @@
 NEG = -1e30
 EPS = 1e-06
 SCALE = 1.0 / math.sqrt(HD)
+LOG2E = math.log2(math.e)
 
 NZ = 16
 ROWS = 72
 CHIPS = 16
 POS = 8
 BLK = 16
-TOK = 1280
 HALF = 640
 PARTS = ((0, 256), (256, 384))
 MESH = pl.DeviceIdType.MESH
@@ -63,10 +63,14 @@
 
 
 def kernel(
-    hid_ref, qkv_ref, wo_ref, wt_ref, mod_ref, ids_ref, out_ref,
-    w8, wxo, wxq, wout, wqkv, sp, res, ns, xa, xs, qs, kt, vs, tt, carry, tba, tbb, rba, rbb,
-    zs, zr, xsq, xrq, zso, zro, xso, xro, zs8, zr8, xs8, xr8, ls, lr, a_s, a_r, hs, hr, ss, sr, r_s, r_r,
+    hid_hbm, qkv_hbm, wo_ref, wt_ref, mod_ref, ids_ref, out_ref,
+    hid_ref, qkv_ref, idb, idg, w8, wxo, wxq, wout, wqkv, sp, res, ns, xa, xs, qs, kt, vs, tt, carry, tba, tbb, rba, rbb,
+    zs, zr, xsq, xrq, zso, zro, xso, xro, zs8, zr8, xs8, xr8, ls, lr, a_s, a_r, hs, hr, ss, sr, r_s, r_r, is_, ir, in_sem,
 ):
+    get_qkv = pltpu.make_async_copy(qkv_hbm, qkv_ref, in_sem.at[0])
+    get_hid = pltpu.make_async_copy(hid_hbm, hid_ref, in_sem.at[1])
+    get_qkv.start()
+    get_hid.start()
     z, seq = lax.axis_index("dp"), lax.axis_index("seq")
     core, chip = seq % 2, seq // 2
     x, y = chip // 4, chip % 4
@@ -119,9 +123,9 @@
         odd = (k // 2) % 2
         return (z, (((x + j * odd) % 4) * 4 + (y + j * (1 - odd)) % 4) * 2 + core)
 
-    def across(k, j):
+    def across(k, j, direct=False):
         ref = wxq.at[quarter(k), k]
-        ahead = k % 2 if j == 1 else 1 - k % 2
+        ahead = 0 if direct else k % 2 if j == 1 else 1 - k % 2
         return copy(ref, ref, xsq, xrq.at[k * ahead + NZ * (1 - ahead)], neighbour(k, j))
 
     def hand_on(k):
@@ -200,10 +204,11 @@
                 ring(way, k).start()
 
     def ring_across(*distances):
-        for j in (1, 3):
+        for j in (2, 1, 3):
             for distance in distances:
                 for way in range(2 if distance < 8 else 1):
-                    across(sent(way, distance), j).start()
+                    if j != 2 or distance >= 7:
+                        across(sent(way, distance), j, distance >= 7).start()
 
     def ring_hand_on(distance):
         for way in range(2 if distance < 8 else 1):
@@ -224,6 +229,16 @@
     for dz in (4, -4):
         ref = wxq.at[quarter(z), z]
         copy(ref, ref, zs, zr.at[z], ((z + dz + NZ) % NZ, seq)).start()
+    first_id, second_id = ids_ref[0].astype(F32), ids_ref[1].astype(F32)
+    idb[core * CHIPS + chip] = jnp.where(iota((BLK, 128), 0) % 2 == 0, first_id, second_id).astype(BF)
+
+    def send_ids(j, _):
+        mine = idb.at[core * CHIPS + chip]
+        copy(mine, mine, is_.at[0], ir.at[0], (z, (seq + j) % 32)).start()
+        return 0
+
+    lax.fori_loop(1, 32, send_ids, 0)
+    get_qkv.wait()
     spatial_pairs(0, 2)
 
     def far(i, _):
@@ -251,6 +266,13 @@
     ring_step(2)
     ring_across(2)
     ring_hand_on(1)
+    others = idb.at[pl.ds(0, 31)]
+    copy(others, others, is_.at[0], ir.at[0], (z, sib)).wait_recv()
+    out_row, in_row = iota((64, 512), 0), iota((64, 512), 1)
+    pick = (in_row == (out_row // 2) * BLK + out_row % 2).astype(F32).astype(BF)
+    idg[1] = dot(pick, idb[...].reshape(512, 128)).astype(BF)
+    copy(idg.at[1], idg.at[0], is_.at[1], ir.at[1], (up, seq)).start()
+    copy(idg.at[1], idg.at[2], is_.at[1], ir.at[2], (down, seq)).start()
     ring_step(5)
     ring_across(5)
     ring_step(3)
@@ -280,6 +302,7 @@
     copy(wxo.at[1 - core], wxo.at[1 - core], ls.at[0], lr.at[0], (z, sib)).wait_recv()
     copy(other, other, ls.at[1], lr.at[1], (z, sib)).wait_recv()
 
+    get_hid.wait()
     for t in range(9):
         piece = w8[...] if t == 8 else wxo[t % 2, t // 2]
         wout[:, 128 * t : 128 * t + 128] = piece.astype(F32).reshape(D, 128).astype(BF)
@@ -292,9 +315,6 @@
 
     def to_owner(d):
         return copy(ns.at[d], xa.at[chip], a_s, a_r.at[chip // 4], (z, d * 2 + core))
-
-    first_id, second_id = ids_ref[0].astype(F32), ids_ref[1].astype(F32)
-    number = jnp.where(iota((BLK, 128), 0) < POS, first_id, second_id).astype(BF)
 
     def norm(step, _):
         i = (step + chip // 2) % 8
@@ -306,8 +326,7 @@
             parts.append(centred * lax.rsqrt(variance + EPS) * (1.0 + mod_ref[2:3, :]) + mod_ref[1:2, :])
         for e in range(2):
             rows = slice(8 * e, 8 * e + 8)
-            ns[2 * i + e, :, 0:D] = jnp.concatenate([parts[0][rows], parts[1][rows]], axis=0).astype(BF)
-            ns[2 * i + e, :, D:TOK] = number
+            ns[2 * i + e] = jnp.concatenate([parts[0][rows], parts[1][rows]], axis=0).astype(BF)
 
             @pl.when(2 * i + e != chip)
             def _():
@@ -344,7 +363,7 @@
             four = ns.at[pl.ds(0, 4)]
             copy(four, four, a_s, a_r.at[g], (z, sib)).wait_recv()
 
-        xs[1, core, g] = dot(sort, xa[pl.ds(4 * g, 4)].reshape(64, TOK)).astype(BF)
+        xs[1, core, g] = dot(sort, xa[pl.ds(4 * g, 4)].reshape(64, D)).astype(BF)
         spread(g)
 
     own_batch(0)
@@ -355,10 +374,8 @@
     own_batch(2)
     ring_hand_on(6)
     own_batch(3)
-    ring_hand_on(7)
-    ring_hand_on(8)
-
-    pieces = wxq.at[pl.ds(0, 2), pl.ds(0, NZ - 1)]
+
+    pieces = wxq.at[pl.ds(0, 3), pl.ds(0, 11)]
     copy(pieces, pieces, xsq, xrq.at[NZ], (z, sib)).wait_recv()
     for q in range(4):
         for u in range(4):
@@ -372,26 +389,25 @@
             there = batch(group, 1 - core, g)
             copy(there, there, ss, sr.at[group, g], (z, sib)).wait_recv()
 
-    def project(groups, low, wide):
-        rows = [xs[group, :, :, :, 0:D].reshape(512, D) for group in groups]
-        return dot(jnp.concatenate(rows, axis=0) if len(rows) > 1 else rows[0], wqkv[:, low : low + wide])
-
-    def keys_values(groups, first_key):
-        keys = slice(first_key, first_key + 64 * len(groups))
+    def project(rows, low, wide):
+        return dot(rows, wqkv[:, low : low + wide])
+
+    def keys_values(rows, first_key):
+        keys = slice(first_key, first_key + rows.shape[0] // POS)
         for low, wide in ((0, 256), (256, 256), (512, 128)):
-            made = project(groups, HALF + low, wide)
+            made = project(rows, HALF + low, wide)
             for p in range(POS):
                 kt[p, low : low + wide, keys] = by_position(made, p).T.astype(BF)
-            made = project(groups, 2 * HALF + low, wide)
+            made = project(rows, 2 * HALF + low, wide)
             for p in range(POS):
                 vs[p, keys, low : low + wide] = by_position(made, p).astype(BF)
 
     wait_sib(1)
     for low, wide in ((0, 256), (256, 256), (512, 128)):
-        made = project((1,), low, wide)
+        made = project(xs[1].reshape(512, D), low, wide)
         for p in range(POS):
             qs[64 * p : 64 * p + 64, low : low + wide] = by_position(made, p).astype(BF)
-    keys_values((1,), 128)
+    keys_values(xs[1].reshape(512, D), 128)
 
     def relay(group, g):
         got = batch(group, core, g)
@@ -404,15 +420,13 @@
             relay(group, g).start()
     for group in (0, 2):
         wait_sib(group)
-    keys_values((0, 2), 0)
+    keys_values(jnp.concatenate([xs[0].reshape(512, D), xs[2].reshape(512, D)], axis=0), 0)
 
     lane = iota((64, 128), 1)
-    def ids_of(group):
-        first = xs[group, :, :, 0:16, D:TOK].astype(F32)
-        return jnp.concatenate([first[b // 4, b % 4, 0:8] for b in range(8)], axis=0)
-
-    ids_q = ids_of(1)
-    ids_k = jnp.concatenate([ids_of(0), ids_of(2), ids_q], axis=0)
+    for way, group in ((0, 0), (1, 2)):
+        copy(idg.at[group], idg.at[group], is_.at[1], ir.at[1 + way], (z, sib)).wait_recv()
+    ids_q = idg[1].astype(F32)
+    ids_k = jnp.concatenate([idg[0], idg[2], idg[1]], axis=0).astype(F32)
     left = jnp.where(lane == 0, ids_q, jnp.where(lane == 1, 1.0, 0.0)).astype(BF)
     lane3 = iota((192, 128), 1)
     right = jnp.where(lane3 == 0, 1.0, jnp.where(lane3 == 1, -ids_k, 0.0)).astype(BF)
@@ -445,8 +459,9 @@
                 rows = pl.ds(pl.multiple_of(64 * p, 64), 64)
                 q = qs[rows, lanes]
                 both = jnp.concatenate([q * first_one, q * second_one], axis=0)
-                scores = jnp.where(same, dot(both, kt[p, lanes, :]) * SCALE, NEG)
-                o = dot(softmax(scores), vs[p, :, lanes])
+                scores = jnp.where(same, dot(both, kt[p, lanes, :]) * (SCALE * LOG2E), NEG)
+                powers = jnp.exp2(scores - jnp.max(scores, axis=-1, keepdims=True))
+                o = dot((powers * (1.0 / jnp.sum(powers, axis=-1, keepdims=True))).astype(BF), vs[p, :, lanes])
                 made = jnp.where(first, o[:64], jnp.where(second, o[64:], 0.0))
                 low = made[:, :128]
                 if i > 0:
@@ -519,6 +534,8 @@
     drain(ns.at[pl.ds(0, 15)], a_s)
     drain(xs.at[0], hs)
     drain(xs.at[pl.ds(0, 3), 0], ss)
+    drain(idb.at[pl.ds(0, 31)], is_.at[0])
+    drain(idg.at[pl.ds(0, 2)], is_.at[1])
     drain(rba.at[pl.ds(0, 31)], r_s.at[0])
     drain(rbb.at[pl.ds(0, 31)], r_s.at[1])
 
@@ -529,9 +546,13 @@
     return pl.pallas_call(
         kernel,
         out_shape=jax.ShapeDtypeStruct(hidden_states.shape, BF),
-        in_specs=[vmem] * 5 + [pl.BlockSpec(memory_space=pltpu.SMEM)],
+        in_specs=[pl.BlockSpec(memory_space=pl.ANY)] * 2 + [vmem] * 3 + [pl.BlockSpec(memory_space=pltpu.SMEM)],
         out_specs=vmem,
         scratch_shapes=[
+            pltpu.VMEM((2, 128, D), BF),
+            pltpu.VMEM((2, 128, 3 * D), BF),
+            pltpu.VMEM((32, BLK, 128), BF),
+            pltpu.VMEM((3, 64, 128), BF),
             pltpu.VMEM((NZ, ROWS, 128), BF),
             pltpu.VMEM((2, 4, NZ, ROWS, 128), BF),
             pltpu.VMEM((4, NZ, ROWS, 512), BF),
@@ -539,9 +560,9 @@
             pltpu.VMEM((D, 2048), BF),
             pltpu.VMEM((256, D), BF),
             pltpu.VMEM((256, D), BF),
-            pltpu.VMEM((CHIPS, BLK, TOK), BF),
-            pltpu.VMEM((CHIPS, BLK, TOK), BF),
-            pltpu.VMEM((3, 2, 4, 64, TOK), BF),
+            pltpu.VMEM((CHIPS, BLK, D), BF),
+            pltpu.VMEM((CHIPS, BLK, D), BF),
+            pltpu.VMEM((3, 2, 4, 64, D), BF),
             pltpu.VMEM((512, HALF), BF),
             pltpu.VMEM((POS, HALF, 192), BF),
             pltpu.VMEM((POS, 192, HALF), BF),
@@ -572,6 +593,9 @@
             dma,
             dma((3, 4)),
             dma((2,)),
+            dma((2,)),
+            dma((2,)),
+            dma((3,)),
             dma((2,)),
         ],
         compiler_params=pltpu.CompilerParams(

time: 105 us -> 103 us (0.981)
  Pallas kernels: 103 us -> 101 us
    pallas_call x1, Pallas kernels: 103 us -> 101 us  [shards(): pl.pallas_call(kernel, out_shape=jax.ShapeDtypeStruct(hidden_states.shape...]
where the time goes in v3:
time: 103 us
  Pallas kernels  101 us (98%)
  local copies, waits for them, and re-layouts  1.92 us (2%)
    pallas_call x1, Pallas kernels, shards(): pl.pallas_call(kernel, out_shape=jax.ShapeDtypeStruct(hidden_states.shape...  101 us

profile of v3, /device:TPU:1, one launch (start us, length us, event | category | flops | bytes accessed | tf_op | source)
XLA Modules:
  0.0 102.9 jit_solution(17756257101547582411)
XLA Ops:
  0.0 101.0 %shard_map.64 = bf16[2,128,1152]{2,1,0:T(8,128)(2,1)} custom-call(bf16[2,128,1152]{2,1,0:T(8,128)(2,1)} %hid_hbm.1, bf16[2,128,3456]{2,1,0:T(8,128)(2,1)} %qkv_hbm.1, bf16[72,1152]{1,0:T(8,128)(2,1)} %wo_ref.1, bf16[72,3456]{1,0:T(8,128)(2,1)} %wt_ref.1, f32[4,1152]{1,0:T(4,128)} %mod_ref.1, s32[2]{0:T(128)} %ids_ref.1), custom_call_target="tpu_custom_call" | custom-call | flops 7000000000 | bytes 5000000 | tf_op jit(solution)/shard_map/pallas_call | solution.py:546
  101.0 1.9 %copy.8 = bf16[2,128,1152]{2,1,0:T(8,128)(2,1)} copy(bf16[2,128,1152]{2,1,0:T(8,128)(2,1)} %shard_map.64) | data formatting | bytes 1179648

commit v4 on v3

--- a/solution.py
+++ b/solution.py
@@ -40,8 +40,9 @@
 
 
 def softmax(scores):
+    scores = scores * (SCALE * LOG2E)
     top = jnp.max(scores, axis=-1, keepdims=True)
-    powers = jnp.exp(scores - top)
+    powers = jnp.exp2(scores - top)
     return (powers * (1.0 / jnp.sum(powers, axis=-1, keepdims=True))).astype(BF)
 
 
@@ -177,24 +178,21 @@
             last_along(k, 1).wait_recv()
 
     def spatial_pair(f, pair):
-        off = pl.multiple_of(128 * pair, 128)
+        off = 128 * pair
         first, second = pair_masks(pair, 128)
         q = qkv_ref[f, :, pl.ds(off, 256)]
-        k = qkv_ref[f, :, pl.ds(pl.multiple_of(D + off, 128), 256)]
-        v = qkv_ref[f, :, pl.ds(pl.multiple_of(2 * D + off, 128), 256)]
+        k = qkv_ref[f, :, pl.ds(D + off, 256)]
+        v = qkv_ref[f, :, pl.ds(2 * D + off, 256)]
         both = jnp.concatenate([q * first.astype(F32).astype(BF), q * second.astype(F32).astype(BF)], axis=0)
-        o = dot(softmax(dot_t(both, k) * SCALE), v)
+        o = dot(softmax(dot_t(both, k)), v)
         rows = slice(128 * f, 128 * f + 128)
         old = sp[rows, pl.ds(off, 256)].astype(F32)
         sp[rows, pl.ds(off, 256)] = jnp.where(first, o[:128], jnp.where(second, o[128:], old)).astype(BF)
 
     def spatial_pairs(low, high):
-        def one(i, _):
+        for i in range(low, high):
             for f in range(2):
                 spatial_pair(f, i)
-            return 0
-
-        lax.fori_loop(low, high, one, 0)
 
     def ring_step(distance):
         for way in range(2 if distance < 8 else 1):
@@ -226,9 +224,6 @@
     for way in range(2):
         ring(way, z).start()
 
-    for dz in (4, -4):
-        ref = wxq.at[quarter(z), z]
-        copy(ref, ref, zs, zr.at[z], ((z + dz + NZ) % NZ, seq)).start()
     first_id, second_id = ids_ref[0].astype(F32), ids_ref[1].astype(F32)
     idb[core * CHIPS + chip] = jnp.where(iota((BLK, 128), 0) % 2 == 0, first_id, second_id).astype(BF)
 
@@ -249,6 +244,9 @@
         return 0
 
     lax.fori_loop(0, 3, far, 0)
+    for dz in (4, -4):
+        ref = wxq.at[quarter(z), z]
+        copy(ref, ref, zs, zr.at[z], ((z + dz + NZ) % NZ, seq)).start()
     ring_step(1)
     ring_across(1)
     spatial_pairs(2, 6)
@@ -259,10 +257,9 @@
         send_across(k)
         return 0
 
-    lax.fori_loop(0, 8, rest, 0)
+    lax.fori_loop(0, 12, rest, 0)
     ring_step(4)
     ring_across(4)
-    lax.fori_loop(8, 12, rest, 0)
     ring_step(2)
     ring_across(2)
     ring_hand_on(1)
@@ -275,9 +272,6 @@
     copy(idg.at[1], idg.at[2], is_.at[1], ir.at[2], (down, seq)).start()
     ring_step(5)
     ring_across(5)
-    ring_step(3)
-    ring_across(3)
-    ring_hand_on(4)
 
     def wait_last(k, _):
         @pl.when((k != z) & (k // 8 == core) & (quarter(k) != (k // 2) % 4))
@@ -295,10 +289,13 @@
     last_to_sib = copy(mine, mine, ls.at[1], lr.at[1], (z, sib))
     last_to_sib.start()
     spatial_pairs(6, 7)
+    ring_step(3)
+    ring_across(3)
+    ring_hand_on(4)
+    spatial_pairs(7, 8)
     ring_step(6)
     ring_across(6)
     ring_hand_on(2)
-    spatial_pairs(7, 8)
     copy(wxo.at[1 - core], wxo.at[1 - core], ls.at[0], lr.at[0], (z, sib)).wait_recv()
     copy(other, other, ls.at[1], lr.at[1], (z, sib)).wait_recv()
 
@@ -317,7 +314,7 @@
         return copy(ns.at[d], xa.at[chip], a_s, a_r.at[chip // 4], (z, d * 2 + core))
 
     def norm(step, _):
-        i = (step + chip // 2) % 8
+        i = (step + 2 * (chip // 4)) % 8
         parts = []
         for f in range(2):
             v = res[pl.ds(pl.multiple_of(128 * f + 16 * i, 16), 16), :].astype(F32)
@@ -352,17 +349,13 @@
         copy(here, batch(2, core, g), hs, hr.at[1, g], (down, seq)).start()
         copy(here, here, ss, sr.at[1, g], (z, sib)).start()
 
-    def own_batch(g):
-        @pl.when(chip // 4 == g)
-        def _():
-            three = ns.at[pl.ds(0, 3)]
-            copy(three, three, a_s, a_r.at[g], (z, sib)).wait_recv()
-
-        @pl.when(chip // 4 != g)
-        def _():
-            four = ns.at[pl.ds(0, 4)]
-            copy(four, four, a_s, a_r.at[g], (z, sib)).wait_recv()
-
+    def turn(i):
+        return (chip // 4 + 4 - i) % 4
+
+    def own_batch(i):
+        g = turn(i)
+        blocks = ns.at[pl.ds(0, 3 if i == 0 else 4)]
+        copy(blocks, blocks, a_s, a_r.at[g], (z, sib)).wait_recv()
         xs[1, core, g] = dot(sort, xa[pl.ds(4 * g, 4)].reshape(64, D)).astype(BF)
         spread(g)
 
@@ -413,7 +406,8 @@
         got = batch(group, core, g)
         return copy(got, got, ss, sr.at[group, g], (z, sib))
 
-    for g in range(4):
+    for i in range(4):
+        g = turn(i)
         for way, group in ((0, 0), (1, 2)):
             got = batch(group, core, g)
             copy(got, got, hs, hr.at[way, g], (z, sib)).wait_recv()

time: 103 us -> 99.1 us (0.962)
  Pallas kernels: 101 us -> 97 us
    pallas_call x1, Pallas kernels: 101 us -> 97 us  [shards(): pl.pallas_call(kernel, out_shape=jax.ShapeDtypeStruct(hidden_states.shape...]
where the time goes in v4:
time: 99.1 us; the launch traced here: 98.9 us
  Pallas kernels  97 us (98%)
  local copies, waits for them, and re-layouts  1.92 us (2%)
    pallas_call x1, Pallas kernels, shards(): pl.pallas_call(kernel, out_shape=jax.ShapeDtypeStruct(hidden_states.shape...  97 us

profile of v4, /device:TPU:1, one launch (start us, length us, event | category | flops | bytes accessed | tf_op | source)
XLA Modules:
  0.0 98.9 jit_solution(2178424539954055915)
XLA Ops:
  0.0 97.0 %shard_map.64 = bf16[2,128,1152]{2,1,0:T(8,128)(2,1)} custom-call(bf16[2,128,1152]{2,1,0:T(8,128)(2,1)} %hid_hbm.1, bf16[2,128,3456]{2,1,0:T(8,128)(2,1)} %qkv_hbm.1, bf16[72,1152]{1,0:T(8,128)(2,1)} %wo_ref.1, bf16[72,3456]{1,0:T(8,128)(2,1)} %wt_ref.1, f32[4,1152]{1,0:T(4,128)} %mod_ref.1, s32[2]{0:T(128)} %ids_ref.1), custom_call_target="tpu_custom_call" | custom-call | flops 7000000000 | bytes 5000000 | tf_op jit(solution)/shard_map/pallas_call | solution.py:540
  97.0 1.9 %copy.8 = bf16[2,128,1152]{2,1,0:T(8,128)(2,1)} copy(bf16[2,128,1152]{2,1,0:T(8,128)(2,1)} %shard_map.64) | data formatting | bytes 1179648
